TPU v7x, 32 devices: a whole 2x2x4 slice. The times are simulated.
32 devices in a mesh: dp: 8 (over y, x, core), owner: 4 (over z).
Axes of the slice: x: 2, y: 2, z: 4, core: 2. Of those that a mesh axis runs over, the one named last changes fastest.
Arguments:
- line_columns: bfloat16 [4, 16384, 512], P(None, ('dp', 'owner')), may hold values from -12 to 12
- line_widths: int32 [32, 4], P(('dp', 'owner')), may hold values from 1 to 128, as said below
- layer_owner: int32 [4], replicated, may hold values from 0 to 3, each once
Outputs:
- preconditioned: float32 [4, 1152, 128], replicated
Inputs may be any that keep to these rules, and one draw needn't show every extreme that they name: `line_widths`: row b holds the widths of the 4 lines of device b, laid end to end from its first position; in every draw the lines of some device all have width 128.
All inputs are finite; a program needn't handle non-finite values.
Results may differ from a plain program's by a relative error of at most 0.0003.
Values may be sent and summed in bfloat16 or wider, within the bound.
A program may use at most 128 MiB of HBM per device.

v0:
```python
import jax
import jax.numpy as jnp
from jax import lax
from jax.sharding import PartitionSpec as P

damping = 0.1


def patch_columns(block, widths):
    positions = block.shape[-2]
    channels = block.shape[-1] // 4
    line_ends = jnp.cumsum(widths, axis=-1).astype(jnp.int32)
    line_starts = line_ends - widths
    place = jnp.arange(positions, dtype=jnp.int32)[:, None]
    opening = jnp.any(place == line_starts[..., None, :], axis=-1)[..., None]
    closing = jnp.any(place + 1 == line_ends[..., None, :], axis=-1)[..., None]
    inside = place < line_ends[..., None, -1:]
    features = block[..., : 3 * channels]
    gradients = block[..., 3 * channels :]
    padding = jnp.zeros_like(features[..., :1, :])
    before = jnp.concatenate([padding, features[..., :-1, :]], axis=-2)
    after = jnp.concatenate([features[..., 1:, :], padding], axis=-2)
    before = jnp.where(opening, jnp.zeros_like(before), before)
    after = jnp.where(closing, jnp.zeros_like(after), after)
    stacked = jnp.concatenate([before, features, after, gradients], axis=-1)
    return jnp.where(inside, stacked, jnp.zeros_like(stacked))


def precondition(factor, total_rows):
    full_width = factor.shape[0]
    patch_width = full_width // 10 * 9
    scaled = factor / total_rows
    act_factor = scaled[:patch_width, :patch_width] + damping * jnp.eye(
        patch_width, dtype=factor.dtype
    )
    grad_factor = scaled[patch_width:, patch_width:] + damping * jnp.eye(
        full_width - patch_width, dtype=factor.dtype
    )
    cross_term = scaled[:patch_width, patch_width:]
    act_cholesky = jnp.linalg.cholesky(act_factor)
    left_solved = jax.scipy.linalg.cho_solve((act_cholesky, True), cross_term)
    grad_cholesky = jnp.linalg.cholesky(grad_factor)
    return jax.scipy.linalg.cho_solve((grad_cholesky, True), left_solved.T).T


def body(line_columns, line_widths, layer_owner):
    layer_count, positions, packed_width = line_columns.shape
    channels = packed_width // 4
    full_width = 10 * channels
    n_replicas = lax.axis_size("dp")
    n_owners = lax.axis_size("owner")
    per_owner = layer_count // n_owners
    total_rows = n_replicas * n_owners * positions
    ordered = jnp.take(line_columns, layer_owner, axis=0)
    width_copies = jnp.broadcast_to(line_widths[None, :, :], (n_owners, 1, line_widths.shape[1]))
    received, source_widths = (
        lax.all_to_all(ordered, "owner", split_axis=0, concat_axis=1, tiled=True),
        lax.all_to_all(width_copies, "owner", split_axis=0, concat_axis=1, tiled=True),
    )
    blocks = received.reshape(per_owner, n_owners, positions, packed_width)
    columns = patch_columns(blocks, source_widths.reshape(n_owners, line_widths.shape[1]))
    columns = columns.reshape(per_owner, n_owners * positions, full_width)
    row_sums = lax.psum_scatter(
        jnp.einsum("lpr,lpb->rlb", columns, columns, preferred_element_type=jnp.float32),
        "dp",
        scatter_dimension=0,
        tiled=True,
    )
    gathered = lax.all_gather(row_sums, "dp", axis=0, tiled=True)
    factors = [gathered[:, 0, :]]
    results = jnp.stack([precondition(factor, total_rows) for factor in factors])
    return lax.all_gather(results, "owner", axis=0, tiled=True)


def solution(mesh):
    in_specs = (P(None, ("dp", "owner"), None), P(("dp", "owner"), None), P())
    out_specs = P()
    return jax.shard_map(body, mesh=mesh, in_specs=in_specs, out_specs=out_specs, check_vma=False)
```

profile of v0, /device:TPU:0, one launch (start us, length us, event | category | flops | bytes accessed | tf_op | source)
XLA Modules:
  0.0 767.0 jit_solution(11130730219817266401)
XLA Ops:
  7.9 6.3 all-to-all-start
  17.6 3.2 broadcast_select_fusion
  20.8 5.1 all-to-all-start.1
  26.5 47.0 %all-to-all-done.1 = bf16[4,512,512]{2,1,0:T(8,128)(2,1)S(1)} async-done(((bf16[4,512,512]{2,1,0:T(8,128)(2,1)}), bf16[4,512,512]{2,1,0:T(8,128)(2,1)S(1)}, u32[]{:S(2)}, u32[]{:S(2)}) %all-to-all-start.1) | async-done | bytes 2097184 | tf_op jit(solution)/shard_map/all_to_all | solution.py:57
  75.7 10.4 %convolution_bitcast_fusion = f32[1280,1,1280]{0,2,1:T(8,128)} fusion(bf16[2048,128]{1,0:T(8,128)(2,1)S(1)} %bitcast.187, bf16[2048,384]{1,0:T(8,128)(2,1)S(1)} %bitcast.185, bf16[2048,384]{1,0:T(8,128)(2,1)S(1)} %bitcast.184, bf16[2048,384]{1,0:T(8,128)(2,1)S(1)} %bitcast.186, pred[2048]{0:T(1024)(128)(4,1)S(1)} %bitcast.190), kind=kOutput, calls=%fused_computation.3 | convolution fusion | flops 6734479360 | bytes 11798528 | tf_op jit(solution)/shard_map/lpr,lpb->rlb/dot_general | solution.py:64
  86.1 14.2 %copy.163 = f32[1280,1,1280]{2,1,0:T(1,128)} copy(f32[1280,1,1280]{0,2,1:T(8,128)} %convolution_bitcast_fusion) | data formatting | bytes 13107200 | tf_op jit(solution)/shard_map/lpr,lpb->rlb/transpose | solution.py:64
  102.2 104.5 %all-reduce.6.cloned.1.call-done = f32[1280,1,1280]{2,1,0:T(1,128)} async-done(((f32[1280,1,1280]{2,1,0:T(1,128)}), f32[1280,1,1280]{2,1,0:T(1,128)}) %all-reduce.6.cloned.1.call-update) | async-done | bytes 6553616
  206.7 2.6 constant_dynamic-slice_fusion.1
  209.4 46.8 %all-gather.4.cloned.1.call-done = f32[1280,1,1280]{2,1,0:T(1,128)} async-done(((f32[160,1,1280]{2,1,0:T(1,128)}), f32[1280,1,1280]{2,1,0:T(1,128)}) %all-gather.4.cloned.1.call-update) | async-done | bytes 6553616 | tf_op jit(solution)/shard_map/all_gather | solution.py:69
  256.2 14.2 %copy.164 = f32[1280,1,1280]{0,2,1:T(8,128)} copy(f32[1280,1,1280]{2,1,0:T(1,128)} %all-gather.4.cloned.1.call-done) | data formatting | bytes 13107200 | tf_op jit(solution)/shard_map/all_gather | solution.py:69
  270.4 3.3 multiply_bitcast_fusion
  273.7 2.7 copy-done.2
  276.5 2.7 slice_add_fusion
  279.2 7.0 copy.170
  286.3 4.6 fusion
  290.9 2.4 copy-done.4
  293.3 11.7 %cholesky.228 = f32[128,128]{1,0:T(8,128)S(1)} custom-call(f32[128,128]{1,0:T(8,128)S(1)} %cholesky.596), custom_call_target="Cholesky" | custom-call | tf_op jit(solution)/shard_map/jit(cholesky)/cholesky | solution.py:40
  305.3 9.8 %custom-call.85 = f32[1,128,128]{1,2,0:T(8,128)S(1)} custom-call(f32[1,128,128]{2,1,0:T(8,128)S(1)} %copy.173), custom_call_target="InvertDiagBlocksLowerTriangular" | custom-call | tf_op jit(solution)/shard_map/jit(cholesky)/cholesky | solution.py:40
  319.4 2.6 cholesky.254
  322.1 12.1 %cholesky.247 = f32[128,128]{1,0:T(8,128)S(1)} custom-call(f32[128,128]{1,0:T(8,128)S(1)} %cholesky.600), custom_call_target="Cholesky" | custom-call | tf_op jit(solution)/shard_map/jit(cholesky)/cholesky | solution.py:40
  337.2 9.8 %custom-call.86 = f32[1,128,128]{1,2,0:T(8,128)S(1)} custom-call(f32[1,128,128]{2,1,0:T(8,128)S(1)} %copy.179), custom_call_target="InvertDiagBlocksLowerTriangular" | custom-call | tf_op jit(solution)/shard_map/jit(cholesky)/cholesky | solution.py:40
  348.4 3.0 convolution_subtract_fusion.1
  351.4 11.7 %cholesky.464 = f32[128,128]{1,0:T(8,128)S(1)} custom-call(f32[128,128]{1,0:T(8,128)S(1)} %cholesky.605), custom_call_target="Cholesky" | custom-call | tf_op jit(solution)/shard_map/jit(cholesky)/cholesky | solution.py:40
  364.6 9.8 %custom-call.87 = f32[1,128,128]{1,2,0:T(8,128)S(1)} custom-call(f32[1,128,128]{2,1,0:T(8,128)S(1)} %copy.184), custom_call_target="InvertDiagBlocksLowerTriangular" | custom-call | tf_op jit(solution)/shard_map/jit(cholesky)/cholesky | solution.py:40
  375.7 3.7 convolution_subtract_fusion.2
  379.5 11.7 %cholesky.483 = f32[128,128]{1,0:T(8,128)S(1)} custom-call(f32[128,128]{1,0:T(8,128)S(1)} %cholesky.610), custom_call_target="Cholesky" | custom-call | tf_op jit(solution)/shard_map/jit(cholesky)/cholesky | solution.py:40
  392.8 9.8 %custom-call.88 = f32[1,128,128]{1,2,0:T(8,128)S(1)} custom-call(f32[1,128,128]{2,1,0:T(8,128)S(1)} %copy.189), custom_call_target="InvertDiagBlocksLowerTriangular" | custom-call | tf_op jit(solution)/shard_map/jit(cholesky)/cholesky | solution.py:40
  403.8 3.7 fusion.13
  407.5 11.9 %cholesky.502 = f32[128,128]{1,0:T(8,128)S(1)} custom-call(f32[128,128]{1,0:T(8,128)S(1)} %cholesky.615), custom_call_target="Cholesky" | custom-call | tf_op jit(solution)/shard_map/jit(cholesky)/cholesky | solution.py:40
  421.0 9.8 %custom-call.89 = f32[1,128,128]{1,2,0:T(8,128)S(1)} custom-call(f32[1,128,128]{2,1,0:T(8,128)S(1)} %copy.194), custom_call_target="InvertDiagBlocksLowerTriangular" | custom-call | tf_op jit(solution)/shard_map/jit(cholesky)/cholesky | solution.py:40
  431.9 3.8 fusion.19
  435.7 11.7 %cholesky.522 = f32[128,128]{1,0:T(8,128)S(1)} custom-call(f32[128,128]{1,0:T(8,128)S(1)} %cholesky.620), custom_call_target="Cholesky" | custom-call | tf_op jit(solution)/shard_map/jit(cholesky)/cholesky | solution.py:40
  449.0 10.2 %custom-call.90 = f32[1,128,128]{1,2,0:T(8,128)S(1)} custom-call(f32[1,128,128]{2,1,0:T(8,128)S(1)} %copy.199), custom_call_target="InvertDiagBlocksLowerTriangular" | custom-call | tf_op jit(solution)/shard_map/jit(cholesky)/cholesky | solution.py:40
  460.3 3.4 fusion.22
  463.8 11.7 %cholesky.542 = f32[128,128]{1,0:T(8,128)S(1)} custom-call(f32[128,128]{1,0:T(8,128)S(1)} %cholesky.625), custom_call_target="Cholesky" | custom-call | tf_op jit(solution)/shard_map/jit(cholesky)/cholesky | solution.py:40
  477.0 9.8 %custom-call.91 = f32[1,128,128]{1,2,0:T(8,128)S(1)} custom-call(f32[1,128,128]{2,1,0:T(8,128)S(1)} %copy.204), custom_call_target="InvertDiagBlocksLowerTriangular" | custom-call | tf_op jit(solution)/shard_map/jit(cholesky)/cholesky | solution.py:40
  487.8 3.0 convolution_subtract_fusion.3
  490.8 11.9 %cholesky.562 = f32[128,128]{1,0:T(8,128)S(1)} custom-call(f32[128,128]{1,0:T(8,128)S(1)} %cholesky.630), custom_call_target="Cholesky" | custom-call | tf_op jit(solution)/shard_map/jit(cholesky)/cholesky | solution.py:40
  504.2 9.8 %custom-call.92 = f32[1,128,128]{1,2,0:T(8,128)S(1)} custom-call(f32[1,128,128]{2,1,0:T(8,128)S(1)} %copy.209), custom_call_target="InvertDiagBlocksLowerTriangular" | custom-call | tf_op jit(solution)/shard_map/jit(cholesky)/cholesky | solution.py:40
  514.9 2.3 convolution_subtract_fusion.16
  517.2 11.7 %cholesky.580 = f32[128,128]{1,0:T(8,128)S(1)} custom-call(f32[128,128]{1,0:T(8,128)S(1)} %convolution_subtract_fusion.16), custom_call_target="Cholesky" | custom-call | tf_op jit(solution)/shard_map/jit(cholesky)/cholesky | solution.py:40
  536.0 5.3 select_select_fusion
  541.3 27.0 %while.1 = (s32[]{:T(128)}, f32[1152,1152]{0,1:T(8,128)}, s32[9,2]{0,1:T(2,128)S(1)}, f32[9,128,128]{2,1,0:T(8,128)S(1)}, s32[]{:T(128)}) while((s32[]{:T(128)}, f32[1152,1152]{0,1:T(8,128)}, s32[9,2]{0,1:T(2,128)S(1)}, f32[9,128,128]{2,1,0:T(8,128)S(1)}, s32[]{:T(128)}) %tuple.71), condition=%wide.while_cond, body=%wide.while_body.sunk | while | flops 2 | bytes 393321 | solution.py:41
  568.3 88.6 %custom-call.93 = f32[9,128,128]{1,2,0:T(8,128)S(1)} custom-call(f32[9,128,128]{2,1,0:T(8,128)S(1)} %get-tuple-element.12), custom_call_target="InvertDiagBlocksLowerTriangular" | custom-call | tf_op jit(solution)/shard_map/jit(_cho_solve)/triangular_solve | solution.py:41
  680.1 11.9 %cholesky.219 = f32[128,128]{1,0:T(8,128)S(1)} custom-call(f32[128,128]{1,0:T(8,128)S(1)} %copy.166), custom_call_target="Cholesky" | custom-call | tf_op jit(solution)/shard_map/jit(cholesky)/cholesky | solution.py:42
  693.7 9.8 %custom-call.84 = f32[1,128,128]{1,2,0:T(8,128)S(1)} custom-call(f32[1,128,128]{2,1,0:T(8,128)S(1)} %copy.169), custom_call_target="InvertDiagBlocksLowerTriangular" | custom-call | tf_op jit(solution)/shard_map/jit(_cho_solve)/triangular_solve | solution.py:43
  706.2 50.6 %all-gather.6.cloned.1.call-done = f32[4608,128]{1,0:T(8,128)} async-done(((f32[1152,128]{1,0:T(8,128)}), f32[4608,128]{1,0:T(8,128)}) %all-gather.6.cloned.1.call-update) | async-done | bytes 2359312 | tf_op jit(solution)/shard_map/all_gather | solution.py:72
  756.8 3.2 copy.320
  (212 shorter events, 88.7 us)
Async XLA Ops:
  6.5 9.0 %copy-start = (bf16[4,512,512]{2,1,0:T(8,128)(2,1)S(1)}, bf16[4,512,512]{2,1,0:T(8,128)(2,1)}, u32[]{:S(2)}) copy-start(bf16[4,512,512]{2,1,0:T(8,128)(2,1)} %param.3) | copy-start | bytes 6291460
  7.9 12.8 %all-to-all-start = ((s32[4,1,4]{2,1,0:T(1,128)}), s32[4,1,4]{2,1,0:T(1,128)S(1)}, u32[]{:S(2)}, u32[]{:S(2)}) async-start(s32[4,1,4]{2,1,0:T(1,128)} %broadcast_in_dim.57), calls=%async_computation | async-start | bytes 4096 | tf_op jit(solution)/shard_map/all_to_all | solution.py:58
  20.8 52.7 %all-to-all-start.1 = ((bf16[4,512,512]{2,1,0:T(8,128)(2,1)}), bf16[4,512,512]{2,1,0:T(8,128)(2,1)S(1)}, u32[]{:S(2)}, u32[]{:S(2)}) async-start(bf16[4,512,512]{2,1,0:T(8,128)(2,1)} %broadcast_select_fusion), calls=%async_computation.1 | async-start | bytes 4194304 | tf_op jit(solution)/shard_map/all_to_all | solution.py:57
  25.9 180.8 %all-reduce.6.cloned.1.call-start = ((), (), s32[]{:S(2)}) async-start(), calls=%async_computation.4 | async-start | bytes 13107200
  100.3 0.7 copy-start.5
  100.3 155.9 %all-gather.4.cloned.1.call-start = ((), (), s32[]{:S(2)}) async-start(), calls=%async_computation.2 | async-start | bytes 7372800 | tf_op jit(solution)/shard_map/all_gather | solution.py:69
  209.3 547.5 %all-gather.6.cloned.1.call-start = ((), (), s32[]{:S(2)}) async-start(), calls=%async_computation.3 | async-start | bytes 2949120 | tf_op jit(solution)/shard_map/all_gather | solution.py:72
  273.7 2.7 copy-start.2
  290.9 2.4 copy-start.4
  656.9 10.2 %copy-start.3 = (f32[1152,1152]{0,1:T(8,128)S(1)}, f32[1152,1152]{0,1:T(8,128)}, u32[]{:S(2)}) copy-start(f32[1152,1152]{0,1:T(8,128)} %get-tuple-element.160) | copy-start | bytes 15925252
  678.1 82.0 %copy-start.1 = (bf16[4,512,512]{2,1,0:T(8,128)(2,1)S(1)}, bf16[4,512,512]{2,1,0:T(8,128)(2,1)}, u32[]{:S(2)}) copy-start(bf16[4,512,512]{2,1,0:T(8,128)(2,1)} %param.3) | copy-start | bytes 6291460
Sparse Core Ops, SparseCore 0:
  100.5 106.1 all-reduce.5
  209.4 46.7 all-gather.3
  706.3 50.4 all-gather.5
where the time goes:
time: 778 us; the launch traced here: 767 us
  other arithmetic  332 us (43%)
  waiting for transfers between devices  249 us (32%)
  local copies, waits for them, and re-layouts  84.5 us (11%)
  matrix products  68.6 us (9%)
  between operations  20.9 us (3%)
  starting transfers between devices  11.5 us (1%)
    another operation x35, other arithmetic, precondition(): act_cholesky = jnp.linalg.cholesky(act_factor)  196 us
    unnamed x4, waiting for transfers between devices  105 us
    another operation x3, other arithmetic, precondition(): left_solved = jax.scipy.linalg.cho_solve((act_cholesky, True), cross_term)  93.9 us
    all_gather x1, waiting for transfers between devices, body(): return lax.all_gather(results, 'owner', axis=0, tiled=True)  50.6 us
    all_to_all x1, waiting for transfers between devices, body(): lax.all_to_all(ordered, 'owner', split_axis=0, concat_axis=1, tiled=True)  47 us
    all_gather x1, waiting for transfers between devices, body(): gathered = lax.all_gather(row_sums, 'dp', axis=0, tiled=True)  46.8 us
    another operation x16, matrix products, precondition(): act_cholesky = jnp.linalg.cholesky(act_factor)  34.1 us
    another operation x45, local copies, waits for them, and re-layouts  26.7 us
  transfers between devices with their start and end apart: 5, of which 4 were waited for; matrix products, arithmetic and copies ran while one was open for 1% of the time, Pallas kernels for 0%

commit v1 on v0

v1 whole, which is shorter than its diff:
```python
import functools

import jax
import jax.numpy as jnp
from jax import lax
from jax.experimental import pallas as pl
from jax.experimental.pallas import tpu as pltpu
from jax.sharding import PartitionSpec as P

damping = 0.1
tile = 128
HIGHEST = lax.Precision.HIGHEST


def invert_tile(matrix):
    groups = tile // 8
    rows = [matrix[8 * i:8 * i + 8, :] for i in range(groups)]
    lane = lax.broadcasted_iota(jnp.int32, (8, tile), 1)
    sub = lax.broadcasted_iota(jnp.int32, (8, tile), 0)
    for p in range(groups):
        low = 8 * p
        in_panel = (lane >= low) & (lane < low + 8)
        unit = jnp.where(lane - low == sub, 1.0, 0.0)
        panel = jnp.where(in_panel, unit, rows[p])
        pivot = [jnp.broadcast_to(rows[p][:, low + j:low + j + 1], (8, tile)) for j in range(8)]
        for j in range(8):
            inverse = 1.0 / pivot[j][j:j + 1, :]
            for m in range(j + 1, 8):
                scaled = pivot[m][j:j + 1, :] * inverse
                pivot[m] = jnp.where(sub == j, scaled, pivot[m] - pivot[j] * scaled)
            scaled = panel[j:j + 1, :] * inverse
            panel = jnp.where(sub == j, scaled, panel - pivot[j] * scaled)
        for i in range(groups):
            if i == p:
                continue
            total = jnp.where(in_panel, 0.0, rows[i])
            for j in range(8):
                column = jnp.broadcast_to(rows[i][:, low + j:low + j + 1], (8, tile))
                total = total - column * panel[j:j + 1, :]
            rows[i] = total
        rows[p] = panel
    return jnp.concatenate(rows, axis=0)


def dot(a, b):
    return jnp.dot(a, b, precision=HIGHEST, preferred_element_type=jnp.float32)


def solve_kernel(scale, gram_ref, out_ref, work, solved):
    packed = gram_ref.shape[0]
    ch = packed // 4
    feat = 3 * ch
    n = 3 * feat
    blocks = n // tile
    first, second, third = packed, 2 * packed, 2 * packed + feat
    fourth = third + feat

    def gram(rows, cols):
        return gram_ref[rows, cols] * scale

    xs = slice(0, feat)
    eye = jnp.where(
        lax.broadcasted_iota(jnp.int32, (feat, feat), 0)
        == lax.broadcasted_iota(jnp.int32, (feat, feat), 1), damping, 0.0)
    centre = gram(xs, slice(0, feat)) + eye
    ahead = gram(xs, slice(first, first + feat))
    work[...] = jnp.zeros_like(work)
    work[0:feat, 0:feat] = centre - gram(xs, slice(third, fourth))
    work[0:feat, feat:2 * feat] = ahead
    work[0:feat, 2 * feat:n] = gram(xs, slice(second, third))
    work[feat:2 * feat, feat:2 * feat] = centre
    work[feat:2 * feat, 2 * feat:n] = ahead
    work[2 * feat:n, 2 * feat:n] = centre - gram(xs, slice(fourth, fourth + feat))
    work[0:feat, n:n + ch] = gram(xs, slice(first + feat, first + packed))
    work[feat:2 * feat, n:n + ch] = gram(xs, slice(feat, packed))
    work[2 * feat:n, n:n + ch] = gram(slice(feat, packed), slice(first, first + feat)).T
    work[n:n + ch, 0:ch] = gram(slice(feat, packed), slice(feat, packed)) + eye[:ch, :ch]

    def eliminate(j, carry):
        top = pl.ds(pl.multiple_of(j * tile, tile), tile)
        col = pl.multiple_of(jnp.where(j == blocks, 0, j) * tile, tile)
        inverse = invert_tile(work[top, pl.ds(col, tile)])

        @pl.when(j < blocks)
        def _():
            row = dot(inverse, work[top, :])
            solved[top, :] = row

            def update(i, carry):
                where = pl.ds(pl.multiple_of(i * tile, tile), tile)
                work[where, :] -= dot(work[top, where].T, solved[top, :])
                return carry

            lax.fori_loop(j + 1, blocks, update, 0)

        @pl.when(j == blocks)
        def _():
            solved[top, 0:tile] = inverse

        return carry

    lax.fori_loop(0, blocks + 1, eliminate, 0)

    out_ref[...] = jnp.zeros_like(out_ref)

    def back(step, carry):
        j = blocks - 1 - step
        top = pl.ds(pl.multiple_of(j * tile, tile), tile)
        out_ref[top, :] = solved[top, n:n + ch] - dot(solved[top, 0:n], out_ref[...])
        return carry

    lax.fori_loop(0, blocks, back, 0)
    out_ref[...] = dot(out_ref[...], solved[n:n + ch, 0:ch])


def precondition(gram, total_rows):
    packed = gram.shape[0]
    ch = packed // 4
    n = 9 * ch
    return pl.pallas_call(
        functools.partial(solve_kernel, 1.0 / total_rows),
        out_shape=jax.ShapeDtypeStruct((n, ch), jnp.float32),
        in_specs=[pl.BlockSpec(memory_space=pltpu.VMEM)],
        out_specs=pl.BlockSpec(memory_space=pltpu.VMEM),
        scratch_shapes=[
            pltpu.VMEM((n + ch, n + ch), jnp.float32),
            pltpu.VMEM((n + ch, n + ch), jnp.float32),
        ],
        compiler_params=pltpu.CompilerParams(vmem_limit_bytes=48 * 2 ** 20),
    )(gram)


def line_masks(widths, positions):
    ends = jnp.cumsum(widths, axis=-1).astype(jnp.int32)
    starts = ends - widths
    place = jnp.arange(positions, dtype=jnp.int32)[:, None]
    inside = place < ends[..., None, -1:]
    opening = jnp.any(place == starts[..., None, :], axis=-1, keepdims=True)
    closing = jnp.any(place + 1 == ends[..., None, :], axis=-1, keepdims=True)
    return inside, opening, closing


def shifted(block):
    return jnp.concatenate([block[..., 1:, :], jnp.zeros_like(block[..., :1, :])], axis=-2)


def body(line_columns, line_widths, layer_owner):
    layer_count, positions, packed = line_columns.shape
    ch = packed // 4
    feat = 3 * ch
    n_replicas = lax.axis_size("dp")
    n_owners = lax.axis_size("owner")
    total_rows = n_replicas * n_owners * positions
    ordered = jnp.take(line_columns, layer_owner, axis=0)
    width_copies = jnp.broadcast_to(line_widths[None, :, :], (n_owners, 1, line_widths.shape[1]))
    received = lax.all_to_all(ordered, "owner", split_axis=0, concat_axis=1, tiled=True)
    source_widths = lax.all_to_all(width_copies, "owner", split_axis=0, concat_axis=1, tiled=True)
    blocks = received.reshape(n_owners, positions, packed)
    inside, opening, closing = line_masks(source_widths.reshape(n_owners, -1), positions)
    zero = jnp.zeros((), blocks.dtype)
    live = jnp.where(inside, blocks, zero)
    ahead = jnp.where(closing, zero, shifted(live))
    ahead2 = jnp.where(closing, zero, shifted(ahead[..., :feat]))
    last = jnp.where(closing, live[..., :feat], zero)
    start = jnp.where(opening & inside, live[..., :feat], zero)
    right = jnp.concatenate([live, ahead, ahead2, last, start], axis=-1)
    gram = lax.dot_general(
        live.reshape(-1, packed), right.reshape(n_owners * positions, -1),
        (((0,), (0,)), ((), ())), preferred_element_type=jnp.float32)
    gram = lax.psum(gram, "dp")
    result = precondition(gram, total_rows)
    return lax.all_gather(result[None], "owner", axis=0, tiled=True)


def solution(mesh):
    in_specs = (P(None, ("dp", "owner"), None), P(("dp", "owner"), None), P())
    return jax.shard_map(body, mesh=mesh, in_specs=in_specs, out_specs=P(), check_vma=False)
```

time: 778 us -> 311 us (0.40); the launches traced: 767 us -> 311 us
  other arithmetic: 332 us -> 9.5 us
  Pallas kernels: 0 us -> 78.9 us
  local copies, waits for them, and re-layouts: 84.5 us -> 9.95 us
  waiting for transfers between devices: 249 us -> 181 us
  matrix products: 68.6 us -> 6.77 us
    another operation x44 -> x1, other arithmetic: 314 us -> 0.18 us  [line_masks(): ends = jnp.cumsum(widths, axis=-1).astype(jnp.int32)]
    unnamed x4 -> x2, waiting for transfers between devices: 105 us -> 0.03 us
    psum x0 -> x1, waiting for transfers between devices: none -> 83.1 us  [body(): gram = lax.psum(gram, 'dp')]
    pallas_call x0 -> x1, Pallas kernels: none -> 78.9 us  [precondition(): pl.pallas_call(functools.partial(solve_kernel, 1.0 / total_rows), out_sha...]
    another operation x52 -> x0, matrix products: 58.2 us -> none  [the longest x16 34.1 us: precondition(): act_cholesky = jnp.linalg.cholesky(act_factor)]
    all_gather x2 -> x1, waiting for transfers between devices: 97.5 us -> 50.7 us  [body(): return lax.all_gather(result[None], 'owner', axis=0, tiled=True)]
    another operation x81 -> x0, local copies, waits for them, and re-layouts: 32.2 us -> none
    all_gather x1 -> x0, local copies, waits for them, and re-layouts: 14.2 us -> none  [body(): gathered = lax.all_gather(row_sums, 'dp', axis=0, tiled=True)]
  transfers between devices with their start and end apart: 5 -> 4, of which waited for: 4 -> 3; matrix products, arithmetic and copies ran while one was open for 1% -> 2% of each run, Pallas kernels for 0% -> 0%
where the time goes in v1:
time: 311 us
  waiting for transfers between devices  181 us (58%)
  Pallas kernels  78.9 us (25%)
  between operations  13.5 us (4%)
  starting transfers between devices  11.5 us (4%)
  local copies, waits for them, and re-layouts  9.95 us (3%)
  other arithmetic  9.5 us (3%)
  matrix products  6.77 us (2%)
    psum x1, waiting for transfers between devices, body(): gram = lax.psum(gram, 'dp')  83.1 us
    pallas_call x1, Pallas kernels, precondition(): pl.pallas_call(functools.partial(solve_kernel, 1.0 / total_rows), out_sha...  78.9 us
    all_gather x1, waiting for transfers between devices, body(): return lax.all_gather(result[None], 'owner', axis=0, tiled=True)  50.7 us
    all_to_all x1, waiting for transfers between devices, body(): lax.all_to_all(ordered, 'owner', split_axis=0, concat_axis=1, tiled=True)  47.1 us
    dot_general x1, matrix products, body(): lax.dot_general(live.reshape(-1, packed), right.reshape(n_owners * positi...  6.77 us
    all_to_all x1, starting transfers between devices, body(): lax.all_to_all(width_copies, 'owner', split_axis=0, concat_axis=1, tiled=...  6.32 us
  transfers between devices with their start and end apart: 4, of which 3 were waited for; matrix products, arithmetic and copies ran while one was open for 2% of the time, Pallas kernels for 0%

profile of v1, /device:TPU:0, one launch (start us, length us, event | category | flops | bytes accessed | tf_op | source)
XLA Modules:
  0.0 310.9 jit_solution(11234176200255521601)
XLA Ops:
  6.5 0.0 copy-start
  6.5 1.4 broadcast_in_dim.81
  7.9 6.3 %all-to-all-start = ((s32[4,1,4]{2,1,0:T(1,128)}), s32[4,1,4]{2,1,0:T(1,128)S(1)}, u32[]{:S(2)}, u32[]{:S(2)}) async-start(s32[4,1,4]{2,1,0:T(1,128)} %broadcast_in_dim.81), calls=%async_computation | async-start | bytes 4096 | tf_op jit(solution)/shard_map/all_to_all | solution.py:157
  14.2 0.7 compare_and_fusion
  14.9 0.7 compare_select_fusion
  15.6 0.0 copy-done
  15.6 2.0 gather_fusion
  17.6 3.2 %broadcast_select_fusion = bf16[4,512,512]{2,1,0:T(8,128)(2,1)} fusion(bf16[4,512,512]{2,1,0:T(8,128)(2,1)} %gather_fusion, pred[4]{0:T(512)(128)(4,1)S(1)} %compare_and_fusion), kind=kLoop, calls=%fused_computation.3 | loop fusion | flops 1048576 | bytes 4194308 | tf_op jit(solution)/shard_map/jit(_take)/select_n | solution.py:154
  20.7 0.0 all-to-all-done
  20.8 5.1 %all-to-all-start.1 = ((bf16[4,512,512]{2,1,0:T(8,128)(2,1)}), bf16[4,512,512]{2,1,0:T(8,128)(2,1)}, u32[]{:S(2)}, u32[]{:S(2)}) async-start(bf16[4,512,512]{2,1,0:T(8,128)(2,1)} %broadcast_select_fusion), calls=%async_computation.1 | async-start | bytes 4194304 | tf_op jit(solution)/shard_map/all_to_all | solution.py:156
  25.8 0.0 all-reduce.4.cloned.1.call-start
  25.8 0.2 reduce_window_sum.13
  26.0 0.2 slice_reduce_fusion
  26.2 0.1 fusion
  26.3 0.1 compare_reduce_fusion
  26.4 0.1 fusion.2
  26.5 47.1 %all-to-all-done.1 = bf16[4,512,512]{2,1,0:T(8,128)(2,1)} async-done(((bf16[4,512,512]{2,1,0:T(8,128)(2,1)}), bf16[4,512,512]{2,1,0:T(8,128)(2,1)}, u32[]{:S(2)}, u32[]{:S(2)}) %all-to-all-start.1) | async-done | bytes 2097184 | tf_op jit(solution)/shard_map/all_to_all | solution.py:156
  73.6 1.8 constant_dynamic-update-slice_fusion.1
  75.4 0.5 slice.24
  75.9 0.6 constant_dynamic-update-slice_fusion
  76.6 0.4 slice.25
  77.0 0.7 select_dynamic-update-slice_fusion.2
  77.7 0.7 select_dynamic-update-slice_fusion.1
  78.4 0.7 select_dynamic-update-slice_fusion
  79.1 6.8 %convolution_bitcast_fusion = f32[512,2176]{1,0:T(8,128)} fusion(bf16[4,512,512]{2,1,0:T(8,128)(2,1)S(1)} %get-tuple-element.8, bf16[4,512,2176]{2,1,0:T(8,128)(2,1)S(1)} %select_dynamic-update-slice_fusion), kind=kOutput, calls=%fused_computation.1 | convolution fusion | flops 4563402752 | bytes 15466496 | tf_op jit(solution)/shard_map/dot_general | solution.py:167
  85.8 0.0 all-reduce.4.cloned.1.call-update
  85.8 0.0 all-gather.3.cloned.1.call-start
  85.9 83.1 %all-reduce.4.cloned.1.call-done.gram_ref = f32[512,2176]{1,0:T(8,128)} async-done(((f32[512,2176]{1,0:T(8,128)}), f32[512,2176]{1,0:T(8,128)}) %all-reduce.4.cloned.1.call-update) | async-done | bytes 4456464 | tf_op jit(solution)/shard_map/psum | solution.py:170
  169.0 0.0 copy-start.1
  169.0 2.3 copy-done.1
  171.3 78.9 %shard_map.37 = f32[1152,128]{1,0:T(8,128)} custom-call(f32[512,2176]{1,0:T(8,128)S(1)} %copy-done.1), custom_call_target="tpu_custom_call" | custom-call | tf_op jit(solution)/shard_map/pallas_call | solution.py:120
  250.1 0.0 all-gather.3.cloned.1.call-update
  250.2 50.7 %all-gather.3.cloned.1.call-done = f32[4608,128]{1,0:T(8,128)} async-done(((f32[1152,128]{1,0:T(8,128)}), f32[4608,128]{1,0:T(8,128)}) %all-gather.3.cloned.1.call-update) | async-done | bytes 2359312 | tf_op jit(solution)/shard_map/all_gather | solution.py:172
  300.9 3.2 %copy.17 = f32[4,1152,128]{2,1,0:T(8,128)} copy(f32[4,1152,128]{2,1,0:T(8,128)} %bitcast.14) | data formatting | bytes 4718592
  (3 shorter events, 0.0 us)
Async XLA Ops:
  6.5 9.0 %copy-start = (bf16[4,512,512]{2,1,0:T(8,128)(2,1)S(1)}, bf16[4,512,512]{2,1,0:T(8,128)(2,1)}, u32[]{:S(2)}) copy-start(bf16[4,512,512]{2,1,0:T(8,128)(2,1)} %param.3) | copy-start | bytes 6291460
  7.9 12.8 %all-to-all-start = ((s32[4,1,4]{2,1,0:T(1,128)}), s32[4,1,4]{2,1,0:T(1,128)S(1)}, u32[]{:S(2)}, u32[]{:S(2)}) async-start(s32[4,1,4]{2,1,0:T(1,128)} %broadcast_in_dim.81), calls=%async_computation | async-start | bytes 4096 | tf_op jit(solution)/shard_map/all_to_all | solution.py:157
  20.8 52.8 %all-to-all-start.1 = ((bf16[4,512,512]{2,1,0:T(8,128)(2,1)}), bf16[4,512,512]{2,1,0:T(8,128)(2,1)}, u32[]{:S(2)}, u32[]{:S(2)}) async-start(bf16[4,512,512]{2,1,0:T(8,128)(2,1)} %broadcast_select_fusion), calls=%async_computation.1 | async-start | bytes 4194304 | tf_op jit(solution)/shard_map/all_to_all | solution.py:156
  25.8 143.2 %all-reduce.4.cloned.1.call-start = ((), (), s32[]{:S(2)}) async-start(), calls=%async_computation.2 | async-start | bytes 8912896 | tf_op jit(solution)/shard_map/psum | solution.py:170
  85.8 215.0 %all-gather.3.cloned.1.call-start = ((), (), s32[]{:S(2)}) async-start(), calls=%async_computation.3 | async-start | bytes 2949120 | tf_op jit(solution)/shard_map/all_gather | solution.py:172
  169.0 2.3 copy-start.1
Sparse Core Ops, SparseCore 0:
  86.0 83.0 all-reduce.3
  250.3 50.5 all-gather.2

commit v2 on v1

--- a/solution.py
+++ b/solution.py
@@ -46,35 +46,49 @@
     return jnp.dot(a, b, precision=HIGHEST, preferred_element_type=jnp.float32)
 
 
+upper = [(r, c) for r in range(3) for c in range(r, 3)]
+square = [(r, c) for r in range(3) for c in range(3)]
+tiles = (
+    upper + [(r, 3) for r in range(3)] + [(3, 3)]
+    + [(r, c + 4) for r, c in square] + [(r, 7) for r in range(3)] + [(3, c + 4) for c in range(3)]
+    + [(r, c + 8) for r, c in square]
+    + [(r, c + 11) for r, c in upper] + [(r, c + 14) for r, c in upper]
+)
+halves, quarters, share = 2, 4, 6
+place_of = {t: (i // (quarters * share), i // share % quarters, i % share) for i, t in enumerate(tiles)}
+
+
 def solve_kernel(scale, gram_ref, out_ref, work, solved):
-    packed = gram_ref.shape[0]
-    ch = packed // 4
-    feat = 3 * ch
-    n = 3 * feat
-    blocks = n // tile
-    first, second, third = packed, 2 * packed, 2 * packed + feat
-    fourth = third + feat
-
-    def gram(rows, cols):
-        return gram_ref[rows, cols] * scale
-
-    xs = slice(0, feat)
+    ch = tile
+    n = 9 * ch
+    blocks = 9
     eye = jnp.where(
-        lax.broadcasted_iota(jnp.int32, (feat, feat), 0)
-        == lax.broadcasted_iota(jnp.int32, (feat, feat), 1), damping, 0.0)
-    centre = gram(xs, slice(0, feat)) + eye
-    ahead = gram(xs, slice(first, first + feat))
+        lax.broadcasted_iota(jnp.int32, (ch, ch), 0)
+        == lax.broadcasted_iota(jnp.int32, (ch, ch), 1), damping, 0.0)
+
+    def gram(r, c):
+        h, q, s = place_of[(r, c)]
+        return gram_ref[h, q, s] * scale
+
+    def put(r, c, value):
+        work[r * ch:(r + 1) * ch, c * ch:(c + 1) * ch] = value
+
     work[...] = jnp.zeros_like(work)
-    work[0:feat, 0:feat] = centre - gram(xs, slice(third, fourth))
-    work[0:feat, feat:2 * feat] = ahead
-    work[0:feat, 2 * feat:n] = gram(xs, slice(second, third))
-    work[feat:2 * feat, feat:2 * feat] = centre
-    work[feat:2 * feat, 2 * feat:n] = ahead
-    work[2 * feat:n, 2 * feat:n] = centre - gram(xs, slice(fourth, fourth + feat))
-    work[0:feat, n:n + ch] = gram(xs, slice(first + feat, first + packed))
-    work[feat:2 * feat, n:n + ch] = gram(xs, slice(feat, packed))
-    work[2 * feat:n, n:n + ch] = gram(slice(feat, packed), slice(first, first + feat)).T
-    work[n:n + ch, 0:ch] = gram(slice(feat, packed), slice(feat, packed)) + eye[:ch, :ch]
+    for r in range(3):
+        for c in range(r, 3):
+            centre = gram(r, c) + eye if r == c else gram(r, c)
+            put(r, c, centre - gram(r, c + 11))
+            put(r + 3, c + 3, centre)
+            put(r + 6, c + 6, centre - gram(r, c + 14))
+        for c in range(3):
+            ahead = gram(r, c + 4)
+            put(r, c + 3, ahead)
+            put(r + 3, c + 6, ahead)
+            put(r, c + 6, gram(r, c + 8))
+        put(r, 9, gram(r, 7))
+        put(r + 3, 9, gram(r, 3))
+        put(r + 6, 9, gram(3, r + 4).T)
+    put(9, 0, gram(3, 3) + eye)
 
     def eliminate(j, carry):
         top = pl.ds(pl.multiple_of(j * tile, tile), tile)
@@ -114,20 +128,24 @@
 
 
 def precondition(gram, total_rows):
-    packed = gram.shape[0]
-    ch = packed // 4
-    n = 9 * ch
+    n = 9 * tile
     return pl.pallas_call(
         functools.partial(solve_kernel, 1.0 / total_rows),
-        out_shape=jax.ShapeDtypeStruct((n, ch), jnp.float32),
+        out_shape=jax.ShapeDtypeStruct((n, tile), jnp.float32),
         in_specs=[pl.BlockSpec(memory_space=pltpu.VMEM)],
         out_specs=pl.BlockSpec(memory_space=pltpu.VMEM),
         scratch_shapes=[
-            pltpu.VMEM((n + ch, n + ch), jnp.float32),
-            pltpu.VMEM((n + ch, n + ch), jnp.float32),
+            pltpu.VMEM((n + tile, n + tile), jnp.float32),
+            pltpu.VMEM((n + tile, n + tile), jnp.float32),
         ],
         compiler_params=pltpu.CompilerParams(vmem_limit_bytes=48 * 2 ** 20),
     )(gram)
+
+
+def pack_tiles(gram):
+    parts = [gram[r * tile:(r + 1) * tile, c * tile:(c + 1) * tile] for r, c in tiles]
+    parts += [jnp.zeros((tile, tile), gram.dtype)] * (halves * quarters * share - len(tiles))
+    return jnp.stack(parts).reshape(halves, quarters, share, tile, tile)
 
 
 def line_masks(widths, positions):
@@ -167,11 +185,288 @@
     gram = lax.dot_general(
         live.reshape(-1, packed), right.reshape(n_owners * positions, -1),
         (((0,), (0,)), ((), ())), preferred_element_type=jnp.float32)
-    gram = lax.psum(gram, "dp")
+    gram = lax.psum(pack_tiles(gram), "dp")
     result = precondition(gram, total_rows)
     return lax.all_gather(result[None], "owner", axis=0, tiled=True)
 
 
+def device(column, core, z):
+    return {"dp": 2 * column + core, "owner": z}
+
+
+def send(src, dst, sems, slot, to):
+    return pltpu.make_async_remote_copy(
+        src_ref=src, dst_ref=dst, send_sem=sems.at[0, slot], recv_sem=sems.at[1, slot],
+        device_id=to, device_id_type=pl.DeviceIdType.MESH)
+
+
+def here():
+    index = lax.axis_index("dp")
+    return index // 2, index % 2, lax.axis_index("owner")
+
+
+def greet(partners):
+    barrier = pltpu.get_barrier_semaphore()
+    for partner in partners:
+        pl.semaphore_signal(barrier, inc=1, device_id=partner, device_id_type=pl.DeviceIdType.MESH)
+    return barrier
+
+
+def block_products(rows_ref, info_ref, gram, first):
+    positions, packed = rows_ref.shape
+    feat = packed // 4 * 3
+    place = lax.broadcasted_iota(jnp.int32, (positions, tile), 0)
+    info = info_ref[...]
+    lines = info.shape[0] // 2
+
+    def any_of(rows, at):
+        hit = at == info[rows[0]:rows[0] + 1, :]
+        for r in rows[1:]:
+            hit = hit | (at == info[r:r + 1, :])
+        return hit
+
+    inside = place < info[2 * lines - 1:2 * lines, :]
+    opening = any_of(range(lines), place) & inside
+    closing = any_of(range(lines, 2 * lines), place + 1)
+
+    def mask(flag, width):
+        return jnp.tile(jnp.where(flag, 1.0, 0.0), (1, width // tile))
+
+    def up(value):
+        return pltpu.roll(value, positions - 1, 0)
+
+    inner = mask(inside & ~closing, packed)
+    live = rows_ref[...].astype(jnp.float32) * mask(inside, packed)
+    ahead = up(live) * inner
+    ahead2 = up(ahead[:, :feat]) * inner[:, :feat]
+    last = live[:, :feat] * mask(closing, feat)
+    start = live[:, :feat] * mask(opening, feat)
+    left = live.astype(jnp.bfloat16).T
+    at = 0
+    for part in (live, ahead, ahead2, last, start):
+        cols = slice(at, at + part.shape[1])
+        product = jnp.dot(left, part.astype(jnp.bfloat16), preferred_element_type=jnp.float32)
+        if first:
+            gram[:, cols] = product
+        else:
+            gram[:, cols] += product
+        at += part.shape[1]
+
+
+def reduce_kernel(rows_ref, info_ref, full, rows_in, info_in, gram, part, core_in, acc,
+                  right_out, left_out, right_in, left_in,
+                  row_sems, info_sems, core_sems, right_sems, left_sems,
+                  ahead_sems, behind_sems, share_sems):
+    column, core, z = here()
+    top = quarters - 1
+    peers = [device(column ^ k, core, z) for k in (1, 2, 3)]
+    sibling = device(column, 1 - core, z)
+    right, left = device(column, core, z + 1), device(column, core, z - 1)
+    barrier = greet(peers + [sibling])
+
+    @pl.when(z < top)
+    def _():
+        pl.semaphore_signal(barrier, inc=1, device_id=right, device_id_type=pl.DeviceIdType.MESH)
+
+    @pl.when(z > 0)
+    def _():
+        pl.semaphore_signal(barrier, inc=1, device_id=left, device_id_type=pl.DeviceIdType.MESH)
+
+    pl.semaphore_wait(barrier, 4 + jnp.where(z < top, 1, 0) + jnp.where(z > 0, 1, 0))
+
+    rows_out = []
+    for k in (1, 2, 3):
+        note = send(info_ref, info_in.at[k - 1], info_sems, k - 1, peers[k - 1])
+        note.start()
+        copy = send(rows_ref.at[column ^ k], rows_in.at[k - 1], row_sems, k - 1, peers[k - 1])
+        copy.start()
+        rows_out.append((note, copy))
+    block_products(rows_ref.at[column], info_ref, gram, True)
+    for k in (1, 2, 3):
+        for copy in rows_out[k - 1]:
+            copy.wait_recv()
+        block_products(rows_in.at[k - 1], info_in.at[k - 1], gram, False)
+
+    for t, (h, q, s) in place_of.items():
+        r, c = t
+        part[h, q, s] = gram[r * tile:(r + 1) * tile, c * tile:(c + 1) * tile]
+    for i in range(len(tiles), halves * quarters * share):
+        part[i // (quarters * share), i // share % quarters, i % share] = jnp.zeros((tile, tile), jnp.float32)
+
+    order = (3, 0, 2, 1)
+    core_out = {}
+    for q in order:
+        core_out[q] = send(part.at[1 - core, q], core_in.at[q], core_sems, q, sibling)
+        core_out[q].start()
+    for q in order:
+        core_out[q].wait_recv()
+        acc[q] = part[core, q] + core_in[q]
+
+    def hop(q, out, into, sems, to):
+        return send(out.at[q], into.at[q], sems, q, to)
+
+    for step in range(top):
+        for q, out, into, sems, to, sends, first in (
+            (top - step, right_out, right_in, right_sems, right, z < top - step, z == 0),
+            (step, left_out, left_in, left_sems, left, z > step, z == top),
+        ):
+            takes = (z > 0) & (z <= q) if out is right_out else (z < top) & (z >= q)
+            copy = hop(q, out, into, sems, to)
+
+            @pl.when(takes)
+            def _(copy=copy):
+                copy.wait_recv()
+
+            @pl.when(sends & first)
+            def _(copy=copy, q=q, out=out):
+                out[q] = acc[q]
+                copy.start()
+
+            @pl.when(sends & ~first)
+            def _(copy=copy, q=q, out=out, into=into):
+                out[q] = acc[q] + into[q]
+                copy.start()
+
+    full[core, z] = acc[z]
+
+    @pl.when(z > 0)
+    def _():
+        full[core, z] += right_in[z]
+
+    @pl.when(z < top)
+    def _():
+        full[core, z] += left_in[z]
+
+    def give(q, sems, to):
+        return send(full.at[core, q], full.at[core, q], sems, q, to)
+
+    def share_with_sibling(q):
+        return send(full.at[core, q], full.at[core, q], share_sems, q, sibling)
+
+    share_with_sibling(z).start()
+    for step in range(top):
+        @pl.when((z < top) & (z - step >= 0))
+        def _(step=step):
+            give(z - step, ahead_sems, right).start()
+
+        @pl.when((z > 0) & (z + step <= top))
+        def _(step=step):
+            give(z + step, behind_sems, left).start()
+
+        @pl.when(z - step - 1 >= 0)
+        def _(step=step):
+            q = z - step - 1
+            give(q, ahead_sems, left).wait_recv()
+            share_with_sibling(q).start()
+
+        @pl.when(z + step + 1 <= top)
+        def _(step=step):
+            q = z + step + 1
+            give(q, behind_sems, right).wait_recv()
+            share_with_sibling(q).start()
+
+    for q in range(quarters):
+        send(full.at[1 - core, q], full.at[1 - core, q], share_sems, q, sibling).wait_recv()
+
+    for pair in rows_out:
+        for copy in pair:
+            copy.wait_send()
+    for q in range(quarters):
+        core_out[q].wait_send()
+        share_with_sibling(q).wait_send()
+
+        @pl.when(z < q)
+        def _(q=q):
+            hop(q, right_out, right_in, right_sems, right).wait_send()
+
+        @pl.when(z > q)
+        def _(q=q):
+            hop(q, left_out, left_in, left_sems, left).wait_send()
+
+        @pl.when((z < top) & (z >= q))
+        def _(q=q):
+            give(q, ahead_sems, right).wait_send()
+
+        @pl.when((z > 0) & (z <= q))
+        def _(q=q):
+            give(q, behind_sems, left).wait_send()
+
+
+def reduced_gram(rows, info):
+    columns, positions, packed = rows.shape
+    wide = 4 * packed + tile
+    quarter = (quarters, share, tile, tile)
+    vmem = pl.BlockSpec(memory_space=pltpu.VMEM)
+    return pl.pallas_call(
+        reduce_kernel,
+        out_shape=jax.ShapeDtypeStruct((halves,) + quarter, jnp.float32),
+        in_specs=[vmem, vmem],
+        out_specs=vmem,
+        scratch_shapes=[
+            pltpu.VMEM((3, positions, packed), rows.dtype),
+            pltpu.VMEM((3,) + info.shape, info.dtype),
+            pltpu.VMEM((packed, wide), jnp.float32),
+            pltpu.VMEM((halves,) + quarter, jnp.float32),
+        ] + [pltpu.VMEM(quarter, jnp.float32)] * 6 + [
+            pltpu.SemaphoreType.DMA((2, 3)),
+            pltpu.SemaphoreType.DMA((2, 3)),
+        ] + [pltpu.SemaphoreType.DMA((2, quarters))] * 6,
+        compiler_params=pltpu.CompilerParams(
+            collective_id=0, has_side_effects=True, vmem_limit_bytes=48 * 2 ** 20),
+    )(rows, info)
+
+
+def spread_kernel(result_ref, out_ref, sems, share_sems):
+    column, core, z = here()
+    n = result_ref.shape[0]
+    rows = n // 2
+    peers = [device(column ^ k, core, z) for k in (1, 2, 3)]
+    sibling = device(column, 1 - core, z)
+    pl.semaphore_wait(greet(peers + [sibling]), 4)
+    mine = pl.ds(pl.multiple_of(core * rows, 8), rows)
+    other = pl.ds(pl.multiple_of((1 - core) * rows, 8), rows)
+    copies = []
+    for k in (1, 2, 3):
+        copy = send(result_ref.at[mine], out_ref.at[column, mine], sems, k - 1, peers[k - 1])
+        copy.start()
+        copies.append(copy)
+    out_ref[column] = result_ref[...]
+    shared = []
+    for k in (1, 2, 3):
+        send(result_ref.at[mine], out_ref.at[column ^ k, mine], sems, k - 1, peers[k - 1]).wait_recv()
+        copy = send(out_ref.at[column ^ k, mine], out_ref.at[column ^ k, mine], share_sems, k - 1, sibling)
+        copy.start()
+        shared.append(copy)
+    for k in (1, 2, 3):
+        part = out_ref.at[column ^ k, other]
+        send(part, part, share_sems, k - 1, sibling).wait_recv()
+        copies[k - 1].wait_send()
+        shared[k - 1].wait_send()
+
+
+def spread(result):
+    vmem = pl.BlockSpec(memory_space=pltpu.VMEM)
+    return pl.pallas_call(
+        spread_kernel,
+        out_shape=jax.ShapeDtypeStruct((4,) + result.shape, result.dtype),
+        in_specs=[vmem],
+        out_specs=vmem,
+        scratch_shapes=[pltpu.SemaphoreType.DMA((2, 3)), pltpu.SemaphoreType.DMA((2, 3))],
+        compiler_params=pltpu.CompilerParams(
+            collective_id=1, has_side_effects=True, vmem_limit_bytes=16 * 2 ** 20),
+    )(result)
+
+
+def direct_body(line_columns, line_widths, layer_owner):
+    total_rows = lax.axis_size("dp") * lax.axis_size("owner") * line_columns.shape[1]
+    ends = jnp.cumsum(line_widths[0])
+    info = jnp.concatenate([ends - line_widths[0], ends]).astype(jnp.int32)
+    info = jnp.broadcast_to(info[:, None], (info.shape[0], tile))
+    gram = reduced_gram(line_columns, info)
+    return jnp.take(spread(precondition(gram, total_rows)), layer_owner, axis=0)
+
+
 def solution(mesh):
     in_specs = (P(None, ("dp", "owner"), None), P(("dp", "owner"), None), P())
-    return jax.shard_map(body, mesh=mesh, in_specs=in_specs, out_specs=P(), check_vma=False)
+    chosen = direct_body if dict(mesh.shape) == {"dp": 8, "owner": 4} else body
+    return jax.shard_map(chosen, mesh=mesh, in_specs=in_specs, out_specs=P(), check_vma=False)

time: 311 us -> 245 us (0.79)
  waiting for transfers between devices: 181 us -> 0 us
  Pallas kernels: 78.9 us -> 236 us
  between operations: 13.5 us -> 0.06 us
  starting transfers between devices: 11.5 us -> 0 us
  matrix products: 6.77 us -> 0 us
  local copies, waits for them, and re-layouts: 9.95 us -> 3.77 us
  other arithmetic: 9.5 us -> 4.87 us
    pallas_call x0 -> x2, Pallas kernels: none -> 158 us  [the longest x1 140 us: reduced_gram(): pl.pallas_call(reduce_kernel, out_shape=jax.ShapeDtypeStruct((halves,) +...]
    psum x1 -> x0, waiting for transfers between devices: 83.1 us -> none  [body(): gram = lax.psum(gram, 'dp')]
    all_gather x1 -> x0, waiting for transfers between devices: 50.7 us -> none  [body(): return lax.all_gather(result[None], 'owner', axis=0, tiled=True)]
    all_to_all x2 -> x0, waiting for transfers between devices: 47.1 us -> none  [the longest x1 47.1 us: body(): lax.all_to_all(ordered, 'owner', split_axis=0, concat_axis=1, tiled=True)]
    all_to_all x2 -> x0, starting transfers between devices: 11.4 us -> none  [the longest x1 6.32 us: body(): lax.all_to_all(width_copies, 'owner', split_axis=0, concat_axis=1, tiled=...]
    dot_general x1 -> x0, matrix products: 6.77 us -> none  [body(): lax.dot_general(live.reshape(-1, packed), right.reshape(n_owners * positi...]
    unnamed x5 -> x4, local copies, waits for them, and re-layouts: 5.49 us -> 1.6 us
    unnamed x4 -> x0, other arithmetic: 3.85 us -> none
  transfers between devices with their start and end apart: 4 -> 0, of which waited for: 3 -> 0; matrix products, arithmetic and copies ran while one was open for 2% -> 0% of each run, Pallas kernels for 0% -> 0%
where the time goes in v2:
time: 245 us
  Pallas kernels  236 us (96%)
  other arithmetic  4.87 us (2%)
  local copies, waits for them, and re-layouts  3.77 us (2%)
    pallas_call x1, Pallas kernels, reduced_gram(): pl.pallas_call(reduce_kernel, out_shape=jax.ShapeDtypeStruct((halves,) +...  140 us
    pallas_call x1, Pallas kernels, precondition(): pl.pallas_call(functools.partial(solve_kernel, 1.0 / total_rows), out_sha...  78 us
    pallas_call x1, Pallas kernels, spread(): pl.pallas_call(spread_kernel, out_shape=jax.ShapeDtypeStruct((4,) + resul...  17.9 us

profile of v2, /device:TPU:0, one launch (start us, length us, event | category | flops | bytes accessed | tf_op | source)
XLA Modules:
  0.0 244.6 jit_solution(3135035877134379017)
XLA Ops:
  0.0 0.8 reduce-window.9
  0.8 0.7 bitcast_subtract_fusion
  1.5 0.1 pad_add_fusion
  1.6 0.1 broadcast_in_dim.19.info_ref
  1.6 0.0 copy-start
  1.6 1.6 copy-done
  3.2 140.0 %shard_map.37.gram_ref = f32[2,4,6,128,128]{4,3,2,1,0:T(8,128)S(1)} custom-call(bf16[4,512,512]{2,1,0:T(8,128)(2,1)S(1)} %copy-done, s32[8,128]{1,0:T(8,128)S(1)} %broadcast_in_dim.19.info_ref), custom_call_target="tpu_custom_call" | custom-call | tf_op jit(solution)/shard_map/pallas_call | solution.py:400
  143.2 78.0 %shard_map.38.result_ref = f32[1152,128]{1,0:T(8,128)S(1)} custom-call(f32[2,4,6,128,128]{4,3,2,1,0:T(8,128)S(1)} %shard_map.37.gram_ref), custom_call_target="tpu_custom_call" | custom-call | tf_op jit(solution)/shard_map/pallas_call | solution.py:132
  221.2 0.0 copy-start.1
  221.2 17.9 %shard_map.39 = f32[4,1152,128]{2,1,0:T(8,128)S(1)} custom-call(f32[1152,128]{1,0:T(8,128)S(1)} %shard_map.38.result_ref), custom_call_target="tpu_custom_call" | custom-call | tf_op jit(solution)/shard_map/pallas_call | solution.py:449
  239.2 0.0 copy-done.1
  239.2 2.1 gather_fusion
  241.3 3.3 %broadcast_select_fusion = f32[4,1152,128]{2,1,0:T(8,128)} fusion(f32[4,1152,128]{2,1,0:T(8,128)} %gather_fusion, pred[4]{0:T(512)(128)(4,1)S(1)} %compare_and_fusion), kind=kLoop, calls=%fused_computation.1 | loop fusion | flops 589824 | bytes 4718596 | tf_op jit(solution)/shard_map/jit(_take)/select_n | solution.py:466
  (3 shorter events, 0.0 us)
Async XLA Ops:
  1.6 1.6 copy-start
  221.2 18.0 %copy-start.1 = (s32[4]{0:T(128)S(1)}, s32[4]{0:T(128)}, u32[]{:S(2)}) copy-start(s32[4]{0:T(128)} %param.5) | copy-start | bytes 52

commit v3 on v2

--- a/solution.py
+++ b/solution.py
@@ -13,16 +13,14 @@
 
 
 def invert_tile(matrix):
-    groups = tile // 8
-    rows = [matrix[8 * i:8 * i + 8, :] for i in range(groups)]
     lane = lax.broadcasted_iota(jnp.int32, (8, tile), 1)
     sub = lax.broadcasted_iota(jnp.int32, (8, tile), 0)
-    for p in range(groups):
-        low = 8 * p
-        in_panel = (lane >= low) & (lane < low + 8)
+    lanes = lax.broadcasted_iota(jnp.int32, (tile, tile), 1)
+    for low in range(0, tile, 8):
+        rows = matrix[low:low + 8, :]
         unit = jnp.where(lane - low == sub, 1.0, 0.0)
-        panel = jnp.where(in_panel, unit, rows[p])
-        pivot = [jnp.broadcast_to(rows[p][:, low + j:low + j + 1], (8, tile)) for j in range(8)]
+        panel = jnp.where((lane >= low) & (lane < low + 8), unit, rows)
+        pivot = [jnp.broadcast_to(rows[:, low + j:low + j + 1], (8, tile)) for j in range(8)]
         for j in range(8):
             inverse = 1.0 / pivot[j][j:j + 1, :]
             for m in range(j + 1, 8):
@@ -30,67 +28,70 @@
                 pivot[m] = jnp.where(sub == j, scaled, pivot[m] - pivot[j] * scaled)
             scaled = panel[j:j + 1, :] * inverse
             panel = jnp.where(sub == j, scaled, panel - pivot[j] * scaled)
-        for i in range(groups):
-            if i == p:
-                continue
-            total = jnp.where(in_panel, 0.0, rows[i])
-            for j in range(8):
-                column = jnp.broadcast_to(rows[i][:, low + j:low + j + 1], (8, tile))
-                total = total - column * panel[j:j + 1, :]
-            rows[i] = total
-        rows[p] = panel
-    return jnp.concatenate(rows, axis=0)
+        total = jnp.where((lanes >= low) & (lanes < low + 8), 0.0, matrix)
+        for j in range(8):
+            total = total - matrix[:, low + j:low + j + 1] * panel[j:j + 1, :]
+        pieces = [total[:low], panel, total[low + 8:]]
+        matrix = jnp.concatenate([piece for piece in pieces if piece.shape[0]], axis=0)
+    return matrix
 
 
 def dot(a, b):
     return jnp.dot(a, b, precision=HIGHEST, preferred_element_type=jnp.float32)
 
 
-upper = [(r, c) for r in range(3) for c in range(r, 3)]
-square = [(r, c) for r in range(3) for c in range(3)]
-tiles = (
-    upper + [(r, 3) for r in range(3)] + [(3, 3)]
-    + [(r, c + 4) for r, c in square] + [(r, 7) for r in range(3)] + [(3, c + 4) for c in range(3)]
-    + [(r, c + 8) for r, c in square]
-    + [(r, c + 11) for r, c in upper] + [(r, c + 14) for r, c in upper]
-)
-halves, quarters, share = 2, 4, 6
-place_of = {t: (i // (quarters * share), i // share % quarters, i % share) for i, t in enumerate(tiles)}
-
-
-def solve_kernel(scale, gram_ref, out_ref, work, solved):
-    ch = tile
-    n = 9 * ch
-    blocks = 9
+triangle = range(3)
+needs = [
+    [(r, c) for c in range(r, 3)] + [(r, c + 4) for c in range(r, 3)]
+    + [(c, r + 4) for c in range(r + 1, 3)] + [(r, 3)] for r in triangle
+] + [
+    [(r, c + 11) for c in range(r, 3)] + [(r, c + 8) for c in triangle] + [(r, 7)] for r in triangle
+] + [
+    [(r, c + 14) for c in range(r, 3)] + [(3, r + 4)] for r in triangle
+] + [[(3, 3)]]
+waves = ((0, 2), (2, 5), (5, 10))
+halves, quarters, share, per_wave = 2, 4, 6, 2
+place_of = {}
+for w, (begin, end) in enumerate(waves):
+    for i, t in enumerate([t for need in needs[begin:end] for t in need]):
+        place_of[t] = (i // (quarters * per_wave), i // per_wave % quarters, per_wave * w + i % per_wave)
+
+
+def add_panel(gram_ref, work, scale, p):
     eye = jnp.where(
-        lax.broadcasted_iota(jnp.int32, (ch, ch), 0)
-        == lax.broadcasted_iota(jnp.int32, (ch, ch), 1), damping, 0.0)
+        lax.broadcasted_iota(jnp.int32, (tile, tile), 0)
+        == lax.broadcasted_iota(jnp.int32, (tile, tile), 1), damping, 0.0)
 
     def gram(r, c):
         h, q, s = place_of[(r, c)]
         return gram_ref[h, q, s] * scale
 
-    def put(r, c, value):
-        work[r * ch:(r + 1) * ch, c * ch:(c + 1) * ch] = value
-
-    work[...] = jnp.zeros_like(work)
-    for r in range(3):
-        for c in range(r, 3):
-            centre = gram(r, c) + eye if r == c else gram(r, c)
-            put(r, c, centre - gram(r, c + 11))
-            put(r + 3, c + 3, centre)
-            put(r + 6, c + 6, centre - gram(r, c + 14))
-        for c in range(3):
-            ahead = gram(r, c + 4)
-            put(r, c + 3, ahead)
-            put(r + 3, c + 6, ahead)
-            put(r, c + 6, gram(r, c + 8))
-        put(r, 9, gram(r, 7))
-        put(r + 3, 9, gram(r, 3))
-        put(r + 6, 9, gram(3, r + 4).T)
-    put(9, 0, gram(3, 3) + eye)
+    def put(c, value):
+        work[p * tile:(p + 1) * tile, c * tile:(c + 1) * tile] += value
+
+    if p == 9:
+        put(0, gram(3, 3) + eye)
+        return
+    tap, r = p // 3, p % 3
+    for c in range(r, 3):
+        centre = gram(r, c) + eye if r == c else gram(r, c)
+        if tap:
+            centre = centre - gram(r, c + (11 if tap == 1 else 14))
+        put(3 * tap + c, centre)
+    for c in range(3):
+        if tap == 0:
+            put(3 + c, gram(c, r + 4).T)
+            put(6 + c, gram(r, c + 4))
+        if tap == 1:
+            put(6 + c, gram(r, c + 8))
+    put(9, gram(3, r + 4).T if tap == 2 else gram(r, 7 if tap == 1 else 3))
+
+
+def eliminate_all(work, solved, prepare):
+    blocks = 9
 
     def eliminate(j, carry):
+        prepare(j)
         top = pl.ds(pl.multiple_of(j * tile, tile), tile)
         col = pl.multiple_of(jnp.where(j == blocks, 0, j) * tile, tile)
         inverse = invert_tile(work[top, pl.ds(col, tile)])
@@ -115,16 +116,28 @@
 
     lax.fori_loop(0, blocks + 1, eliminate, 0)
 
-    out_ref[...] = jnp.zeros_like(out_ref)
-
-    def back(step, carry):
-        j = blocks - 1 - step
-        top = pl.ds(pl.multiple_of(j * tile, tile), tile)
-        out_ref[top, :] = solved[top, n:n + ch] - dot(solved[top, 0:n], out_ref[...])
-        return carry
-
-    lax.fori_loop(0, blocks, back, 0)
-    out_ref[...] = dot(out_ref[...], solved[n:n + ch, 0:ch])
+
+def substitute(solved, answer, tap):
+    n = 9 * tile
+    for j in range(3 * tap + 2, 3 * tap - 1, -1):
+        rows = slice(j * tile, (j + 1) * tile)
+        value = solved[rows, n:n + tile]
+        if j < 8:
+            after = slice((j + 1) * tile, n)
+            value = value - dot(solved[rows, after], answer[after, :])
+        answer[rows, :] = value
+    rows = slice(3 * tap * tile, 3 * (tap + 1) * tile)
+    return dot(answer[rows, :], solved[n:n + tile, 0:tile]), (1, 0, 2)[tap] * 3 * tile
+
+
+def solve_kernel(scale, gram_ref, out_ref, work, solved, answer):
+    work[...] = jnp.zeros_like(work)
+    for p in range(10):
+        add_panel(gram_ref, work, scale, p)
+    eliminate_all(work, solved, lambda j: None)
+    for tap in (2, 1, 0):
+        value, at = substitute(solved, answer, tap)
+        out_ref[at:at + 3 * tile, :] = value
 
 
 def precondition(gram, total_rows):
@@ -137,14 +150,17 @@
         scratch_shapes=[
             pltpu.VMEM((n + tile, n + tile), jnp.float32),
             pltpu.VMEM((n + tile, n + tile), jnp.float32),
+            pltpu.VMEM((n, tile), jnp.float32),
         ],
         compiler_params=pltpu.CompilerParams(vmem_limit_bytes=48 * 2 ** 20),
     )(gram)
 
 
 def pack_tiles(gram):
-    parts = [gram[r * tile:(r + 1) * tile, c * tile:(c + 1) * tile] for r, c in tiles]
-    parts += [jnp.zeros((tile, tile), gram.dtype)] * (halves * quarters * share - len(tiles))
+    filled = {at: gram[r * tile:(r + 1) * tile, c * tile:(c + 1) * tile] for (r, c), at in place_of.items()}
+    empty = jnp.zeros((tile, tile), gram.dtype)
+    parts = [filled.get((h, q, s), empty)
+             for h in range(halves) for q in range(quarters) for s in range(share)]
     return jnp.stack(parts).reshape(halves, quarters, share, tile, tile)
 
 
@@ -253,10 +269,9 @@
         at += part.shape[1]
 
 
-def reduce_kernel(rows_ref, info_ref, full, rows_in, info_in, gram, part, core_in, acc,
+def reduce_kernel(rows_ref, info_ref, mine, rows_in, info_in, gram, part, core_in, acc,
                   right_out, left_out, right_in, left_in,
-                  row_sems, info_sems, core_sems, right_sems, left_sems,
-                  ahead_sems, behind_sems, share_sems):
+                  row_sems, info_sems, core_sems, right_sems, left_sems):
     column, core, z = here()
     top = quarters - 1
     peers = [device(column ^ k, core, z) for k in (1, 2, 3)]
@@ -290,8 +305,11 @@
     for t, (h, q, s) in place_of.items():
         r, c = t
         part[h, q, s] = gram[r * tile:(r + 1) * tile, c * tile:(c + 1) * tile]
-    for i in range(len(tiles), halves * quarters * share):
-        part[i // (quarters * share), i // share % quarters, i % share] = jnp.zeros((tile, tile), jnp.float32)
+    for h in range(halves):
+        for q in range(quarters):
+            for s in range(share):
+                if (h, q, s) not in place_of.values():
+                    part[h, q, s] = jnp.zeros((tile, tile), jnp.float32)
 
     order = (3, 0, 2, 1)
     core_out = {}
@@ -327,53 +345,21 @@
                 out[q] = acc[q] + into[q]
                 copy.start()
 
-    full[core, z] = acc[z]
+    mine[...] = acc[z]
 
     @pl.when(z > 0)
     def _():
-        full[core, z] += right_in[z]
+        mine[...] += right_in[z]
 
     @pl.when(z < top)
     def _():
-        full[core, z] += left_in[z]
-
-    def give(q, sems, to):
-        return send(full.at[core, q], full.at[core, q], sems, q, to)
-
-    def share_with_sibling(q):
-        return send(full.at[core, q], full.at[core, q], share_sems, q, sibling)
-
-    share_with_sibling(z).start()
-    for step in range(top):
-        @pl.when((z < top) & (z - step >= 0))
-        def _(step=step):
-            give(z - step, ahead_sems, right).start()
-
-        @pl.when((z > 0) & (z + step <= top))
-        def _(step=step):
-            give(z + step, behind_sems, left).start()
-
-        @pl.when(z - step - 1 >= 0)
-        def _(step=step):
-            q = z - step - 1
-            give(q, ahead_sems, left).wait_recv()
-            share_with_sibling(q).start()
-
-        @pl.when(z + step + 1 <= top)
-        def _(step=step):
-            q = z + step + 1
-            give(q, behind_sems, right).wait_recv()
-            share_with_sibling(q).start()
-
-    for q in range(quarters):
-        send(full.at[1 - core, q], full.at[1 - core, q], share_sems, q, sibling).wait_recv()
+        mine[...] += left_in[z]
 
     for pair in rows_out:
         for copy in pair:
             copy.wait_send()
     for q in range(quarters):
         core_out[q].wait_send()
-        share_with_sibling(q).wait_send()
 
         @pl.when(z < q)
         def _(q=q):
@@ -383,23 +369,15 @@
         def _(q=q):
             hop(q, left_out, left_in, left_sems, left).wait_send()
 
-        @pl.when((z < top) & (z >= q))
-        def _(q=q):
-            give(q, ahead_sems, right).wait_send()
-
-        @pl.when((z > 0) & (z <= q))
-        def _(q=q):
-            give(q, behind_sems, left).wait_send()
-
-
-def reduced_gram(rows, info):
+
+def reduced_quarter(rows, info):
     columns, positions, packed = rows.shape
     wide = 4 * packed + tile
     quarter = (quarters, share, tile, tile)
     vmem = pl.BlockSpec(memory_space=pltpu.VMEM)
     return pl.pallas_call(
         reduce_kernel,
-        out_shape=jax.ShapeDtypeStruct((halves,) + quarter, jnp.float32),
+        out_shape=jax.ShapeDtypeStruct(quarter[1:], jnp.float32),
         in_specs=[vmem, vmem],
         out_specs=vmem,
         scratch_shapes=[
@@ -410,51 +388,116 @@
         ] + [pltpu.VMEM(quarter, jnp.float32)] * 6 + [
             pltpu.SemaphoreType.DMA((2, 3)),
             pltpu.SemaphoreType.DMA((2, 3)),
-        ] + [pltpu.SemaphoreType.DMA((2, quarters))] * 6,
+        ] + [pltpu.SemaphoreType.DMA((2, quarters))] * 3,
         compiler_params=pltpu.CompilerParams(
             collective_id=0, has_side_effects=True, vmem_limit_bytes=48 * 2 ** 20),
     )(rows, info)
 
 
-def spread_kernel(result_ref, out_ref, sems, share_sems):
+def finish_kernel(scale, mine, out_ref, full, work, solved, answer,
+                  give_sems, share_sems, row_sems, pass_sems):
     column, core, z = here()
-    n = result_ref.shape[0]
-    rows = n // 2
     peers = [device(column ^ k, core, z) for k in (1, 2, 3)]
+    chain = [device(column, core, z ^ k) for k in (1, 2, 3)]
     sibling = device(column, 1 - core, z)
-    pl.semaphore_wait(greet(peers + [sibling]), 4)
-    mine = pl.ds(pl.multiple_of(core * rows, 8), rows)
-    other = pl.ds(pl.multiple_of((1 - core) * rows, 8), rows)
-    copies = []
-    for k in (1, 2, 3):
-        copy = send(result_ref.at[mine], out_ref.at[column, mine], sems, k - 1, peers[k - 1])
-        copy.start()
-        copies.append(copy)
-    out_ref[column] = result_ref[...]
-    shared = []
-    for k in (1, 2, 3):
-        send(result_ref.at[mine], out_ref.at[column ^ k, mine], sems, k - 1, peers[k - 1]).wait_recv()
-        copy = send(out_ref.at[column ^ k, mine], out_ref.at[column ^ k, mine], share_sems, k - 1, sibling)
-        copy.start()
-        shared.append(copy)
-    for k in (1, 2, 3):
-        part = out_ref.at[column ^ k, other]
-        send(part, part, share_sems, k - 1, sibling).wait_recv()
-        copies[k - 1].wait_send()
-        shared[k - 1].wait_send()
-
-
-def spread(result):
+    barrier = greet(peers + chain + [sibling])
+    full[core, z] = mine[...]
+    work[...] = jnp.zeros_like(work)
+    pl.semaphore_wait(barrier, 7)
+
+    def piece(h, q, w):
+        return full.at[h, q, pl.ds(per_wave * w, per_wave)]
+
+    def give(w, k):
+        return send(piece(core, z, w), piece(core, z, w), give_sems, 3 * w + k - 1, chain[k - 1])
+
+    def arriving(w, k):
+        return send(piece(core, z ^ k, w), piece(core, z ^ k, w), give_sems, 3 * w + k - 1, chain[k - 1])
+
+    def share_piece(h, w, k):
+        return send(piece(h, z ^ k, w), piece(h, z ^ k, w), share_sems, 4 * w + k, sibling)
+
+    def begin(w):
+        for k in (3, 2, 1):
+            give(w, k).start()
+        share_piece(core, w, 0).start()
+
+    begin(0)
+
+    def prepare(j):
+        for w, (first, end) in enumerate(waves):
+            @pl.when(j == first)
+            def _(w=w, first=first, end=end):
+                for k in (1, 2, 3):
+                    arriving(w, k).wait_recv()
+                    share_piece(core, w, k).start()
+                if w + 1 < len(waves):
+                    begin(w + 1)
+                for k in range(4):
+                    share_piece(1 - core, w, k).wait_recv()
+                for p in range(first, end):
+                    add_panel(full, work, scale, p)
+
+    eliminate_all(work, solved, prepare)
+
+    half = 3 * tile // 2
+
+    def rows_of(col, side, at):
+        return out_ref.at[col, pl.ds(pl.multiple_of(at + side * half, 8), half)]
+
+    def spread_rows(at, tap, k):
+        part = rows_of(column, core, at)
+        return send(part, part, row_sems, 3 * tap + k - 1, peers[k - 1])
+
+    def pass_rows(side, at, tap, k):
+        part = rows_of(column ^ k, side, at)
+        return send(part, part, pass_sems, 3 * tap + k - 1, sibling)
+
+    order = []
+    for tap in (2, 1, 0):
+        value, at = substitute(solved, answer, tap)
+        out_ref[column, at:at + 3 * tile, :] = value
+        for k in (1, 2, 3):
+            spread_rows(at, tap, k).start()
+        order.append((at, tap))
+    for at, tap in order:
+        for k in (1, 2, 3):
+            part = rows_of(column ^ k, core, at)
+            send(part, part, row_sems, 3 * tap + k - 1, peers[k - 1]).wait_recv()
+            pass_rows(core, at, tap, k).start()
+    for at, tap in order:
+        for k in (1, 2, 3):
+            pass_rows(1 - core, at, tap, k).wait_recv()
+            pass_rows(core, at, tap, k).wait_send()
+            spread_rows(at, tap, k).wait_send()
+    for w in range(len(waves)):
+        for k in (1, 2, 3):
+            give(w, k).wait_send()
+        for k in range(4):
+            share_piece(core, w, k).wait_send()
+
+
+def finish(mine, total_rows):
     vmem = pl.BlockSpec(memory_space=pltpu.VMEM)
+    n = 9 * tile
     return pl.pallas_call(
-        spread_kernel,
-        out_shape=jax.ShapeDtypeStruct((4,) + result.shape, result.dtype),
+        functools.partial(finish_kernel, 1.0 / total_rows),
+        out_shape=jax.ShapeDtypeStruct((4, n, tile), mine.dtype),
         in_specs=[vmem],
         out_specs=vmem,
-        scratch_shapes=[pltpu.SemaphoreType.DMA((2, 3)), pltpu.SemaphoreType.DMA((2, 3))],
+        scratch_shapes=[
+            pltpu.VMEM((halves, quarters, share, tile, tile), jnp.float32),
+            pltpu.VMEM((n + tile, n + tile), jnp.float32),
+            pltpu.VMEM((n + tile, n + tile), jnp.float32),
+            pltpu.VMEM((n, tile), jnp.float32),
+            pltpu.SemaphoreType.DMA((2, 9)),
+            pltpu.SemaphoreType.DMA((2, 12)),
+            pltpu.SemaphoreType.DMA((2, 9)),
+            pltpu.SemaphoreType.DMA((2, 9)),
+        ],
         compiler_params=pltpu.CompilerParams(
-            collective_id=1, has_side_effects=True, vmem_limit_bytes=16 * 2 ** 20),
-    )(result)
+            collective_id=1, has_side_effects=True, vmem_limit_bytes=48 * 2 ** 20),
+    )(mine)
 
 
 def direct_body(line_columns, line_widths, layer_owner):
@@ -462,8 +505,8 @@
     ends = jnp.cumsum(line_widths[0])
     info = jnp.concatenate([ends - line_widths[0], ends]).astype(jnp.int32)
     info = jnp.broadcast_to(info[:, None], (info.shape[0], tile))
-    gram = reduced_gram(line_columns, info)
-    return jnp.take(spread(precondition(gram, total_rows)), layer_owner, axis=0)
+    mine = reduced_quarter(line_columns, info)
+    return jnp.take(finish(mine, total_rows), layer_owner, axis=0)
 
 
 def solution(mesh):

time: 245 us -> 232 us (0.947); the launches traced: 245 us -> 227 us
  Pallas kernels: 236 us -> 218 us
    pallas_call x3 -> x2, Pallas kernels: 236 us -> 218 us  [the longest x1 114 us: finish(): pl.pallas_call(functools.partial(finish_kernel, 1.0 / total_rows), out_sh...]
where the time goes in v3:
time: 232 us; the launch traced here: 227 us
  Pallas kernels  218 us (94%)
  other arithmetic  4.87 us (2%)
  local copies, waits for them, and re-layouts  3.77 us (2%)
    pallas_call x1, Pallas kernels, finish(): pl.pallas_call(functools.partial(finish_kernel, 1.0 / total_rows), out_sh...  114 us
    pallas_call x1, Pallas kernels, reduced_quarter(): pl.pallas_call(reduce_kernel, out_shape=jax.ShapeDtypeStruct(quarter[1:],...  104 us

profile of v3, /device:TPU:0, one launch (start us, length us, event | category | flops | bytes accessed | tf_op | source)
XLA Modules:
  0.0 227.2 jit_solution(12760219849435559778)
XLA Ops:
  0.0 0.8 reduce-window.9
  0.8 0.7 bitcast_subtract_fusion
  1.5 0.1 pad_add_fusion
  1.6 0.1 broadcast_in_dim.19.info_ref
  1.6 0.0 copy-start
  1.6 1.6 copy-done
  3.2 0.0 copy-start.1
  3.2 104.5 %shard_map.37.mine = f32[6,128,128]{2,1,0:T(8,128)S(1)} custom-call(bf16[4,512,512]{2,1,0:T(8,128)(2,1)S(1)} %copy-done, s32[8,128]{1,0:T(8,128)S(1)} %broadcast_in_dim.19.info_ref), custom_call_target="tpu_custom_call" | custom-call | tf_op jit(solution)/shard_map/pallas_call | solution.py:378
  107.7 114.0 %shard_map.38 = f32[4,1152,128]{2,1,0:T(8,128)S(1)} custom-call(f32[6,128,128]{2,1,0:T(8,128)S(1)} %shard_map.37.mine), custom_call_target="tpu_custom_call" | custom-call | tf_op jit(solution)/shard_map/pallas_call | solution.py:483
  221.7 0.0 copy-done.1
  221.8 2.1 gather_fusion
  223.9 3.3 %broadcast_select_fusion = f32[4,1152,128]{2,1,0:T(8,128)} fusion(f32[4,1152,128]{2,1,0:T(8,128)} %gather_fusion, pred[4]{0:T(512)(128)(4,1)S(1)} %compare_and_fusion), kind=kLoop, calls=%fused_computation.1 | loop fusion | flops 589824 | bytes 4718596 | tf_op jit(solution)/shard_map/jit(_take)/select_n | solution.py:509
  (3 shorter events, 0.0 us)
Async XLA Ops:
  1.6 1.6 copy-start
  3.2 218.5 %copy-start.1 = (s32[4]{0:T(128)S(1)}, s32[4]{0:T(128)}, u32[]{:S(2)}) copy-start(s32[4]{0:T(128)} %param.5) | copy-start | bytes 52
